TPU v7x, 256 devices: a whole 4x4x8 slice. The times are simulated.
256 devices in a mesh: dp: 32 (over z, y), tensor: 8 (over x, core).
Axes of the slice: x: 4, y: 4, z: 8, core: 2. Of those that a mesh axis runs over, the one named last changes fastest.
Arguments:
- queries: bfloat16 [96, 256, 8192], P('dp', None, 'tensor'), may hold values from -6 to 6
- response_keys: bfloat16 [96, 256, 1024], P('dp', None, 'tensor'), may hold values from -6 to 6
- response_values: bfloat16 [96, 256, 1024], P('dp', None, 'tensor'), may hold values from -6 to 6
- out_grad: bfloat16 [96, 256, 5120], P('dp', 'tensor'), may hold values from -6 to 6
- advantages: float32 [96, 256], P('dp', 'tensor'), may hold values from -4 to 4
- lengths: int32 [96], P('dp'), may hold values from 128 to 256, as said below
- groups: int32 [96], P('dp'), may hold values from 0 to 31, as said below
- prompt_keys: bfloat16 [32, 256, 1024], P('dp', None, 'tensor'), may hold values from -6 to 6
- prompt_value_rows: bfloat16 [32, 256, 1024], P('dp', None, 'tensor'), may hold values from -6 to 6
- w_out: bfloat16 [5120, 8192], P('dp', 'tensor'), may hold values from -0.078125 to 0.078125
Outputs:
- query_grad: bfloat16 [96, 256, 8192], P('dp', None, 'tensor')
- key_grad: bfloat16 [96, 256, 1024], P('dp', None, 'tensor')
- value_grad: bfloat16 [96, 256, 1024], P('dp', None, 'tensor')
- prompt_key_grad: float32 [32, 256, 1024], P('dp', None, 'tensor')
- prompt_value_grad: float32 [32, 256, 1024], P('dp', None, 'tensor')
Inputs may be any that keep to these rules, and one draw needn't show every extreme that they name: lengths are multiples of 128; some response has 256. groups[s] = (s // 3 + o) mod 32 with o between -2 and 2; both ends of o occur in every draw; the number of responses of a prompt varies.
All inputs are finite; a program needn't handle non-finite values.
Results may differ from a plain program's by a relative error of at most 0.0086.
Values may be sent and summed in bfloat16 or wider, within the bound.
No kernel may reach another device: no remote copies, remote signals or barrier semaphores. Data moves between devices by JAX's collectives and lax.ppermute only.
A program may use at most 128 MiB of HBM per device.

v0:
```python
import jax
import jax.numpy as jnp
from jax import lax
from jax.sharding import PartitionSpec as P

HEAD_SIZE = 128
RESPONSE_LENGTH = 256
SPREAD = 2


loss_scale = 16.0
mask_value = -1e30


def from_behind(block, axis, distance):
    devices = range(lax.axis_size(axis))
    route = [((i - distance) % len(devices), i) for i in devices]
    return lax.ppermute(block, axis, route)


def attend(query_rows, key_rows, value_rows, grad_rows, prompt_len):
    query_len = query_rows.shape[0]
    key_len = key_rows.shape[0]
    kv_heads = key_rows.shape[1] // HEAD_SIZE
    group = query_rows.shape[1] // HEAD_SIZE // kv_heads
    head_scale = HEAD_SIZE ** (-0.5)
    query_heads = query_rows.reshape(query_len, kv_heads, group, HEAD_SIZE)
    key_heads = key_rows.reshape(key_len, kv_heads, HEAD_SIZE)
    value_heads = value_rows.reshape(key_len, kv_heads, HEAD_SIZE)
    grad_heads = grad_rows.reshape(query_len, kv_heads, group, HEAD_SIZE)
    scores = (
        jnp.einsum("qkgd,lkd->kgql", query_heads, key_heads, preferred_element_type=jnp.float32)
        * head_scale
    )
    query_pos = jnp.arange(query_len, dtype=jnp.int32)[:, None]
    key_pos = jnp.arange(key_len, dtype=jnp.int32)[None, :]
    allowed = (key_pos < prompt_len) | (key_pos - prompt_len <= query_pos)
    scores = jnp.where(allowed, scores, mask_value)
    weights = jax.nn.softmax(scores, axis=-1)
    weights_low = weights.astype(jnp.bfloat16)
    dweights = jnp.einsum(
        "qkgd,lkd->kgql", grad_heads, value_heads, preferred_element_type=jnp.float32
    )
    dscores = weights * (dweights - jnp.sum(weights * dweights, axis=-1, keepdims=True))
    dscores_low = dscores.astype(jnp.bfloat16)
    query_grad = (
        jnp.einsum("kgql,lkd->qkgd", dscores_low, key_heads, preferred_element_type=jnp.float32)
        * head_scale
    )
    key_grad = (
        jnp.einsum("kgql,qkgd->lkd", dscores_low, query_heads, preferred_element_type=jnp.float32)
        * head_scale
    )
    value_grad = jnp.einsum(
        "kgql,qkgd->lkd", weights_low, grad_heads, preferred_element_type=jnp.float32
    )
    return (
        query_grad.reshape(query_len, -1).astype(jnp.bfloat16),
        key_grad.reshape(key_len, -1),
        value_grad.reshape(key_len, -1),
    )


def on_device(
    queries,
    response_keys,
    response_values,
    out_grad,
    advantages,
    lengths,
    groups,
    prompt_keys,
    prompt_value_rows,
    w_out,
):
    slots, local_rows, width = out_grad.shape
    prompt_len = prompt_keys.shape[1]
    channels = prompt_keys.shape[2]
    dp_count = lax.axis_size("dp")
    my_index = lax.axis_index("dp")
    positions = lax.axis_index("tensor") * local_rows + jnp.arange(local_rows, dtype=jnp.int32)
    live_mask = jnp.where(positions[None, :] < lengths[:, None], 1.0, 0.0).astype(jnp.float32)
    factor = (
        advantages
        * live_mask
        * (loss_scale * RESPONSE_LENGTH / lengths.astype(jnp.float32))[:, None]
    )
    scaled = (out_grad.astype(jnp.float32) * factor[:, :, None]).astype(jnp.bfloat16)
    gathered = lax.all_gather(scaled, "tensor", axis=1, tiled=True)
    flat_rows = gathered.reshape(slots * RESPONSE_LENGTH, width)
    d_out = jnp.dot(
        flat_rows,
        lax.all_gather(w_out, "dp", axis=0, tiled=True),
        preferred_element_type=jnp.float32,
    )
    d_out = d_out.astype(jnp.bfloat16).reshape(slots, RESPONSE_LENGTH, w_out.shape[1])
    raw_offsets = (groups - my_index) % dp_count
    offsets = jnp.where(raw_offsets > dp_count // 2, raw_offsets - dp_count, raw_offsets)
    tile_pair = jnp.concatenate([prompt_keys, prompt_value_rows], 0)
    arrivals = {0: tile_pair}
    for offset in range(-SPREAD, SPREAD + 1):
        if offset != 0:
            arrivals[offset] = from_behind(tile_pair, "dp", -offset)
    received = jnp.zeros((slots, 2, prompt_len, channels), jnp.bfloat16)
    for offset in range(-SPREAD, SPREAD + 1):
        received = jnp.where(
            (offsets == offset)[:, None, None, None], arrivals[offset][None], received
        )
    taken_keys = received[:, 0]
    taken_values = received[:, 1]

    def per_slot(inputs_one):
        query_rows, own_keys, own_values, key_tile, value_tile, grad_rows = inputs_one
        key_rows = jnp.concatenate([key_tile, own_keys], 0)
        value_rows = jnp.concatenate([value_tile, own_values], 0)
        return attend(query_rows, key_rows, value_rows, grad_rows, prompt_len)

    query_grad, all_key, all_value = lax.map(
        per_slot, (queries, response_keys, response_values, taken_keys, taken_values, d_out)
    )
    key_grad = all_key[:, prompt_len:].astype(jnp.bfloat16)
    value_grad = all_value[:, prompt_len:].astype(jnp.bfloat16)
    prompt_part = jnp.stack([all_key[:, :prompt_len], all_value[:, :prompt_len]], 1)

    def offset_sum(offset):
        chosen = (offsets == offset)[:, None, None, None]
        return jnp.sum(jnp.where(chosen, prompt_part, 0.0), axis=0)

    summed = offset_sum(0)
    for offset in range(-SPREAD, SPREAD + 1):
        if offset != 0:
            summed = summed + from_behind(
                offset_sum(offset).astype(jnp.bfloat16), "dp", offset
            ).astype(jnp.float32)
    summed = summed[None]
    return (query_grad, key_grad, value_grad, summed[:, 0], summed[:, 1])


def solution(mesh):
    in_specs = (
        P("dp", None, "tensor"),
        P("dp", None, "tensor"),
        P("dp", None, "tensor"),
        P("dp", "tensor", None),
        P("dp", "tensor"),
        P("dp"),
        P("dp"),
        P("dp", None, "tensor"),
        P("dp", None, "tensor"),
        P("dp", "tensor"),
    )
    out_specs = (
        P("dp", None, "tensor"),
        P("dp", None, "tensor"),
        P("dp", None, "tensor"),
        P("dp", None, "tensor"),
        P("dp", None, "tensor"),
    )
    return jax.shard_map(
        on_device, mesh=mesh, in_specs=in_specs, out_specs=out_specs, check_vma=False
    )
```

profile of v0, /device:TPU:2, one launch (start us, length us, event | category | flops | bytes accessed | tf_op | source)
XLA Modules:
  0.0 279.8 jit_solution(9115496048604959807)
XLA Ops:
  8.6 2.4 multiply_convert_fusion
  13.5 8.6 %collective-permute-start = (bf16[2,256,128]{2,1,0:T(8,128)(2,1)S(1)}, bf16[2,256,128]{2,1,0:T(8,128)(2,1)S(1)}, u32[]{:S(2)}, u32[]{:S(2)}) collective-permute-start(bf16[2,256,128]{2,1,0:T(8,128)(2,1)S(1)} %constant_dynamic-update-slice_fusion.1), channel_id=1, source_target_pairs={{16,0},{24,8},{32,16},{40,24},{48,32},{56,40},{64,48},{72,56},{80,... | collective-permute-start | bytes 393224 | tf_op jit(solution)/shard_map/ppermute | solution.py:18
  22.1 1.1 collective-permute-start.1
  23.1 1.0 collective-permute-start.2
  26.1 2.3 collective-permute-done.1
  28.6 5.0 %collective-permute-done.2 = bf16[2,256,128]{2,1,0:T(8,128)(2,1)S(1)} collective-permute-done((bf16[2,256,128]{2,1,0:T(8,128)(2,1)S(1)}, bf16[2,256,128]{2,1,0:T(8,128)(2,1)S(1)}, u32[]{:S(2)}, u32[]{:S(2)}) %collective-permute-start.2) | collective-permute-done | bytes 131104 | tf_op jit(solution)/shard_map/ppermute | solution.py:18
  35.0 28.4 %all-gather.3.cloned.1.call-done = bf16[3,256,5120]{2,1,0:T(8,128)(2,1)} async-done(((bf16[3,32,5120]{2,1,0:T(8,128)(2,1)}), bf16[3,256,5120]{2,1,0:T(8,128)(2,1)}) %all-gather.3.cloned.1.call-update) | async-done | bytes 7864336 | tf_op jit(solution)/shard_map/all_gather | solution.py:89
  63.4 112.7 %all-gather.5.cloned.1.call-done = bf16[5120,1024]{1,0:T(8,128)(2,1)} async-done(((bf16[160,1024]{1,0:T(8,128)(2,1)}), bf16[5120,1024]{1,0:T(8,128)(2,1)}) %all-gather.5.cloned.1.call-update) | async-done | bytes 10485776 | tf_op jit(solution)/shard_map/all_gather | solution.py:93
  176.1 14.2 %convolution_convert_fusion = bf16[768,1024]{1,0:T(8,128)(2,1)} fusion(bf16[768,5120]{1,0:T(8,128)(2,1)} %bitcast.179, bf16[5120,1024]{1,0:T(8,128)(2,1)} %all-gather.5.cloned.1.call-done), kind=kOutput, calls=%fused_computation.45 | convolution fusion | flops 8053850112 | bytes 19922944 | tf_op jit(solution)/shard_map/dot_general | solution.py:91
  190.4 65.2 %while.16 = (s32[]{:T(128)}, bf16[3,256,1024]{2,1,0:T(8,128)(2,1)}, f32[3,512,128]{1,2,0:T(8,128)}, f32[3,512,128]{1,2,0:T(8,128)}, bf16[3,256,128]{1,2,0:T(8,12...) while((s32[]{:T(128)}, bf16[3,256,1024]{2,1,0:T(8,128)(2,1)}, ...), condition=%wide.region_4.5_spmd, body=%wide.region_0.4_spmd.sunk | while | flops 1370024960 | bytes 80706224 | solution.py:118
  190.4 1.3 constant_dynamic-slice_fusion.6
  191.8 0.9 constant_dynamic-slice_fusion.7
  192.9 0.9 dynamic-slice_bitcast_fusion.3
  194.8 1.9 copy-done
  196.7 0.9 fusion.64
  197.8 4.2 %fusion.69 = f32[3,512,128]{1,2,0:T(8,128)} fusion(f32[3,512,128]{1,2,0:T(8,128)} %get-tuple-element.322, s32[]{:T(128)} %get-tuple-element.319, bf16[256,8,128]{0,2,1:T(8,128)(2,1)S(1)} %bitcast.176, f32[8,256]{1,0:T(8,128)S(1)} %fusion.64, f32[8,256]{1,0:T(8,128)S(1)} %get-tuple-element.302, f32[512,256,8]{1,0,2:T(8,128)} %copy-done, ...), kind=kOutput, calls=%fused_computation.17.clone.1 | convolution fusion | flops 273678336 | bytes 5128704 | tf_op jit(solution)/shard_map/while/body/eval_jaxpr/kgql,qkgd->lkd/dot_general | solution.py:54
  202.1 3.8 %fusion.65 = (f32[8,256]{1,0:T(8,128)S(1)}, f32[512,256,8]{1,0,2:T(8,128)S(1)}) fusion(f32[8,256]{1,0:T(8,128)S(1)} %fusion.64, f32[8,256]{1,0:T(8,128)S(1)} %get-tuple-element.302, f32[512,256,8]{1,0,2:T(8,128)} %copy-done, pred[256,512]{0,1:T(8,128)(4,1)S(1)} %fusion.62, bf16[256,8,128]{0,2,1:T(8,128)(2,1)S(1)} %bitcast.177, ...), kind=kOutput, calls=%fused_computation.3.clone.1 | convolution fusion | flops 274987008 | bytes 9199616 | tf_op jit(solution)/shard_map/while/body/eval_jaxpr/qkgd,lkd->kgql/dot_general | solution.py:41
  206.0 1.3 fusion.66
  207.3 1.3 fusion.67
  208.5 1.2 copy.91
  210.6 1.5 fusion.68
  212.1 1.3 constant_dynamic-slice_fusion.6
  213.6 0.9 constant_dynamic-slice_fusion.7
  214.6 0.9 dynamic-slice_bitcast_fusion.3
  216.5 1.9 copy-done
  218.4 0.9 fusion.64
  219.5 4.2 %fusion.69 = f32[3,512,128]{1,2,0:T(8,128)} fusion(f32[3,512,128]{1,2,0:T(8,128)} %get-tuple-element.322, s32[]{:T(128)} %get-tuple-element.319, bf16[256,8,128]{0,2,1:T(8,128)(2,1)S(1)} %bitcast.176, f32[8,256]{1,0:T(8,128)S(1)} %fusion.64, f32[8,256]{1,0:T(8,128)S(1)} %get-tuple-element.302, f32[512,256,8]{1,0,2:T(8,128)} %copy-done, ...), kind=kOutput, calls=%fused_computation.17.clone.1 | convolution fusion | flops 273678336 | bytes 5128704 | tf_op jit(solution)/shard_map/while/body/eval_jaxpr/kgql,qkgd->lkd/dot_general | solution.py:54
  223.9 3.8 %fusion.65 = (f32[8,256]{1,0:T(8,128)S(1)}, f32[512,256,8]{1,0,2:T(8,128)S(1)}) fusion(f32[8,256]{1,0:T(8,128)S(1)} %fusion.64, f32[8,256]{1,0:T(8,128)S(1)} %get-tuple-element.302, f32[512,256,8]{1,0,2:T(8,128)} %copy-done, pred[256,512]{0,1:T(8,128)(4,1)S(1)} %fusion.62, bf16[256,8,128]{0,2,1:T(8,128)(2,1)S(1)} %bitcast.177, ...), kind=kOutput, calls=%fused_computation.3.clone.1 | convolution fusion | flops 274987008 | bytes 9199616 | tf_op jit(solution)/shard_map/while/body/eval_jaxpr/qkgd,lkd->kgql/dot_general | solution.py:41
  227.7 1.3 fusion.66
  229.0 1.3 fusion.67
  230.3 1.2 copy.91
  232.3 1.5 fusion.68
  233.9 1.3 constant_dynamic-slice_fusion.6
  235.3 0.9 constant_dynamic-slice_fusion.7
  236.3 0.9 dynamic-slice_bitcast_fusion.3
  238.3 1.9 copy-done
  241.3 4.2 %fusion.69 = f32[3,512,128]{1,2,0:T(8,128)} fusion(f32[3,512,128]{1,2,0:T(8,128)} %get-tuple-element.322, s32[]{:T(128)} %get-tuple-element.319, bf16[256,8,128]{0,2,1:T(8,128)(2,1)S(1)} %bitcast.176, f32[8,256]{1,0:T(8,128)S(1)} %fusion.64, f32[8,256]{1,0:T(8,128)S(1)} %get-tuple-element.302, f32[512,256,8]{1,0,2:T(8,128)} %copy-done, ...), kind=kOutput, calls=%fused_computation.17.clone.1 | convolution fusion | flops 273678336 | bytes 5128704 | tf_op jit(solution)/shard_map/while/body/eval_jaxpr/kgql,qkgd->lkd/dot_general | solution.py:54
  245.6 3.8 %fusion.65 = (f32[8,256]{1,0:T(8,128)S(1)}, f32[512,256,8]{1,0,2:T(8,128)S(1)}) fusion(f32[8,256]{1,0:T(8,128)S(1)} %fusion.64, f32[8,256]{1,0:T(8,128)S(1)} %get-tuple-element.302, f32[512,256,8]{1,0,2:T(8,128)} %copy-done, pred[256,512]{0,1:T(8,128)(4,1)S(1)} %fusion.62, bf16[256,8,128]{0,2,1:T(8,128)(2,1)S(1)} %bitcast.177, ...), kind=kOutput, calls=%fused_computation.3.clone.1 | convolution fusion | flops 274987008 | bytes 9199616 | tf_op jit(solution)/shard_map/while/body/eval_jaxpr/qkgd,lkd->kgql/dot_general | solution.py:41
  249.5 1.3 fusion.66
  250.8 1.3 fusion.67
  252.0 1.2 copy.91
  254.1 1.5 fusion.68
  255.6 1.2 slice_bitcast_fusion
  257.2 2.3 collective-permute-start.4
  259.6 1.4 collective-permute-start.5
  261.6 1.3 collective-permute-start.7
  262.9 1.4 copy.65
  266.0 5.1 %collective-permute-done.6 = bf16[2,256,128]{1,2,0:T(8,128)(2,1)S(1)} collective-permute-done((bf16[2,256,128]{1,2,0:T(8,128)(2,1)S(1)}, bf16[2,256,128]{1,2,0:T(8,128)(2,1)S(1)}, u32[]{:S(2)}, u32[]{:S(2)}) %collective-permute-start.6) | collective-permute-done | bytes 131104 | tf_op jit(solution)/shard_map/ppermute | solution.py:18
  (75 shorter events, 20.2 us)
Async XLA Ops:
  7.2 56.2 %all-gather.3.cloned.1.call-start = ((), (), s32[]{:S(2)}) async-start(), calls=%async_computation | async-start | bytes 8847360 | tf_op jit(solution)/shard_map/all_gather | solution.py:89
  11.1 165.1 %all-gather.5.cloned.1.call-start = ((), (), s32[]{:S(2)}) async-start(), calls=%async_computation.1 | async-start | bytes 10813440 | tf_op jit(solution)/shard_map/all_gather | solution.py:93
  13.5 12.5 %collective-permute-start = (bf16[2,256,128]{2,1,0:T(8,128)(2,1)S(1)}, bf16[2,256,128]{2,1,0:T(8,128)(2,1)S(1)}, u32[]{:S(2)}, u32[]{:S(2)}) collective-permute-start(bf16[2,256,128]{2,1,0:T(8,128)(2,1)S(1)} %constant_dynamic-update-slice_fusion.1), channel_id=1, source_target_pairs={{16,0},{24,8},{32,16},{40,24},{48,32},{56,40},{64,48},{72,56},{80,... | collective-permute-start | bytes 393224 | tf_op jit(solution)/shard_map/ppermute | solution.py:18
  22.1 6.4 %collective-permute-start.1 = (bf16[2,256,128]{2,1,0:T(8,128)(2,1)S(1)}, bf16[2,256,128]{2,1,0:T(8,128)(2,1)S(1)}, u32[]{:S(2)}, u32[]{:S(2)}) collective-permute-start(bf16[2,256,128]{2,1,0:T(8,128)(2,1)S(1)} %constant_dynamic-update-slice_fusion.1), channel_id=1, source_target_pairs={{8,0},{16,8},{24,16},{32,24},{40,32},{48,40},{56,48},{64,56},{72,6... | collective-permute-start | bytes 393224 | tf_op jit(solution)/shard_map/ppermute | solution.py:18
  23.1 10.4 %collective-permute-start.2 = (bf16[2,256,128]{2,1,0:T(8,128)(2,1)S(1)}, bf16[2,256,128]{2,1,0:T(8,128)(2,1)S(1)}, u32[]{:S(2)}, u32[]{:S(2)}) collective-permute-start(bf16[2,256,128]{2,1,0:T(8,128)(2,1)S(1)} %constant_dynamic-update-slice_fusion.1), channel_id=1, source_target_pairs={{248,0},{0,8},{8,16},{16,24},{24,32},{32,40},{40,48},{48,56},{56,6... | collective-permute-start | bytes 393224 | tf_op jit(solution)/shard_map/ppermute | solution.py:18
  24.1 9.8 %collective-permute-start.3 = (bf16[2,256,128]{2,1,0:T(8,128)(2,1)S(1)}, bf16[2,256,128]{2,1,0:T(8,128)(2,1)S(1)}, u32[]{:S(2)}, u32[]{:S(2)}) collective-permute-start(bf16[2,256,128]{2,1,0:T(8,128)(2,1)S(1)} %constant_dynamic-update-slice_fusion.1), channel_id=1, source_target_pairs={{240,0},{248,8},{0,16},{8,24},{16,32},{24,40},{32,48},{40,56},{48,... | collective-permute-start | bytes 393224 | tf_op jit(solution)/shard_map/ppermute | solution.py:18
  194.8 1.9 copy-start
  202.1 3.9 %copy-start.1 = (f32[512,256,8]{1,0,2:T(8,128)S(1)}, f32[512,256,8]{1,0,2:T(8,128)}, u32[]{:S(2)}) copy-start(f32[512,256,8]{1,0,2:T(8,128)} %copy-done) | copy-start | bytes 12582916 | tf_op jit(solution)/shard_map/while
  216.5 1.9 copy-start
  223.8 3.8 %copy-start.1 = (f32[512,256,8]{1,0,2:T(8,128)S(1)}, f32[512,256,8]{1,0,2:T(8,128)}, u32[]{:S(2)}) copy-start(f32[512,256,8]{1,0,2:T(8,128)} %copy-done) | copy-start | bytes 12582916 | tf_op jit(solution)/shard_map/while
  238.2 1.9 copy-start
  245.6 3.8 %copy-start.1 = (f32[512,256,8]{1,0,2:T(8,128)S(1)}, f32[512,256,8]{1,0,2:T(8,128)}, u32[]{:S(2)}) copy-start(f32[512,256,8]{1,0,2:T(8,128)} %copy-done) | copy-start | bytes 12582916 | tf_op jit(solution)/shard_map/while
  255.6 8.6 %copy-start.2 = (f32[3,512,128]{1,2,0:T(8,128)S(1)}, f32[3,512,128]{1,2,0:T(8,128)}, u32[]{:S(2)}) copy-start(f32[3,512,128]{1,2,0:T(8,128)} %get-tuple-element.133) | copy-start | bytes 2359300
  257.2 8.6 %collective-permute-start.4 = (bf16[2,256,128]{1,2,0:T(8,128)(2,1)S(1)}, bf16[2,256,128]{1,2,0:T(8,128)(2,1)S(1)}, u32[]{:S(2)}, u32[]{:S(2)}) collective-permute-start(bf16[2,256,128]{1,2,0:T(8,128)(2,1)S(1)} %get-tuple-element.180), channel_id=1, source_target_pairs={{16,0},{24,8},{32,16},{40,24},{48,32},{56,40},{64,48},{72,56},{80,... | collective-permute-start | bytes 393224 | tf_op jit(solution)/shard_map/ppermute | solution.py:18
  259.6 6.5 %collective-permute-start.5 = (bf16[2,256,128]{1,2,0:T(8,128)(2,1)S(1)}, bf16[2,256,128]{1,2,0:T(8,128)(2,1)S(1)}, u32[]{:S(2)}, u32[]{:S(2)}) collective-permute-start(bf16[2,256,128]{1,2,0:T(8,128)(2,1)S(1)} %get-tuple-element.181), channel_id=1, source_target_pairs={{8,0},{16,8},{24,16},{32,24},{40,32},{48,40},{56,48},{64,56},{72,6... | collective-permute-start | bytes 393224 | tf_op jit(solution)/shard_map/ppermute | solution.py:18
  261.0 10.1 %collective-permute-start.6 = (bf16[2,256,128]{1,2,0:T(8,128)(2,1)S(1)}, bf16[2,256,128]{1,2,0:T(8,128)(2,1)S(1)}, u32[]{:S(2)}, u32[]{:S(2)}) collective-permute-start(bf16[2,256,128]{1,2,0:T(8,128)(2,1)S(1)} %get-tuple-element.182), channel_id=1, source_target_pairs={{248,0},{0,8},{8,16},{16,24},{24,32},{32,40},{40,48},{48,56},{56,6... | collective-permute-start | bytes 393224 | tf_op jit(solution)/shard_map/ppermute | solution.py:18
  261.6 9.8 %collective-permute-start.7 = (bf16[2,256,128]{1,2,0:T(8,128)(2,1)S(1)}, bf16[2,256,128]{1,2,0:T(8,128)(2,1)S(1)}, u32[]{:S(2)}, u32[]{:S(2)}) collective-permute-start(bf16[2,256,128]{1,2,0:T(8,128)(2,1)S(1)} %get-tuple-element.183), channel_id=1, source_target_pairs={{240,0},{248,8},{0,16},{8,24},{16,32},{24,40},{32,48},{40,56},{48,... | collective-permute-start | bytes 393224 | tf_op jit(solution)/shard_map/ppermute | solution.py:18
Sparse Core Ops, SparseCore 0:
  11.2 52.1 all-gather.2
  66.0 110.0 all-gather.4
where the time goes:
time: 281 us; the launch traced here: 280 us
  waiting for transfers between devices  155 us (55%)
  matrix products  49 us (17%)
  local copies, waits for them, and re-layouts  31.8 us (11%)
  starting transfers between devices  17 us (6%)
  between operations  14.2 us (5%)
  other arithmetic  12.2 us (4%)
    all_gather x1, waiting for transfers between devices, on_device(): lax.all_gather(w_out, 'dp', axis=0, tiled=True)  113 us
    all_gather x1, waiting for transfers between devices, on_device(): gathered = lax.all_gather(scaled, 'tensor', axis=1, tiled=True)  28.4 us
    ppermute x8, starting transfers between devices, from_behind(): return lax.ppermute(block, axis, route)  16.9 us
    dot_general x1, matrix products, on_device(): jnp.dot(flat_rows, lax.all_gather(w_out, 'dp', axis=0, tiled=True), prefe...  14.2 us
    ppermute x8, waiting for transfers between devices, from_behind(): return lax.ppermute(block, axis, route)  13.5 us
    dot_general x3, matrix products, attend(): jnp.einsum('kgql,qkgd->lkd', weights_low, grad_heads, preferred_element_t...  12.6 us
    dot_general x3, matrix products, attend(): jnp.einsum('qkgd,lkd->kgql', grad_heads, value_heads, preferred_element_t...  11.5 us
    dynamic_slice x18, local copies, waits for them, and re-layouts, on_device(): lax.map(per_slot, (queries, response_keys, response_values, taken_keys, t...  8.35 us
  transfers between devices with their start and end apart: 10, of which 9 were waited for; matrix products, arithmetic and copies ran while one was open for 2% of the time, Pallas kernels for 0%

commit v1 on v0

v1 whole, which is shorter than its diff:
```python
import functools

import jax
import jax.numpy as jnp
from jax import lax
from jax.experimental import pallas as pl
from jax.experimental.pallas import tpu as pltpu
from jax.sharding import Mesh
from jax.sharding import PartitionSpec as P

HEAD_SIZE = 128
RESPONSE_LENGTH = 256
SPREAD = 2
Y_SIZE = 4
CORES = 2
VMEM_LIMIT = 60 * 2**20

loss_scale = 16.0
mask_value = -1e30
head_scale = HEAD_SIZE ** (-0.5)
F32 = jnp.float32
BF16 = jnp.bfloat16


def shift(block, axis, distance):
    count = lax.axis_size(axis)
    route = [(i, (i + distance) % count) for i in range(count)]
    return lax.ppermute(block, axis, route)


def ring_gather(block, axis, between=None):
    count = lax.axis_size(axis)
    rows = block.shape[0]
    pieces = [(0, 0, block)]
    up = down = block
    for step in range(1, count // 2):
        up = shift(up, axis, 1)
        down = shift(down, axis, -1)
        if between is not None:
            up, down = between(step, pieces, up, down)
        pieces += [(-step, 0, up), (step, 0, down)]
    far = count // 2
    half = rows // 2
    up, down = lax.optimization_barrier((up[:half], down[half:]))
    pieces += [(far, 0, shift(up, axis, 1)), (far, half, shift(down, axis, -1))]
    return pieces


def probs_kernel(q_ref, k_ref, out_ref, *, heads, prompt_len):
    keys = k_ref[0]
    own_len = keys.shape[0] - prompt_len
    query_len = q_ref.shape[1]
    row = lax.broadcasted_iota(jnp.int32, (own_len, query_len), 0)
    col = lax.broadcasted_iota(jnp.int32, (own_len, query_len), 1)
    for h in range(heads):
        q = q_ref[0, :, h * HEAD_SIZE:(h + 1) * HEAD_SIZE]
        scores = lax.dot_general(keys, q, (((1,), (1,)), ((), ())), preferred_element_type=F32) * head_scale
        top = scores[:prompt_len]
        low = jnp.where(row <= col, scores[prompt_len:], mask_value)
        peak = jnp.maximum(jnp.max(top, axis=0, keepdims=True), jnp.max(low, axis=0, keepdims=True))
        top = jnp.exp(top - peak)
        low = jnp.exp(low - peak)
        total = jnp.sum(top, axis=0, keepdims=True) + jnp.sum(low, axis=0, keepdims=True)
        inv = 1.0 / total
        cols = slice(h * query_len, (h + 1) * query_len)
        out_ref[0, :prompt_len, cols] = (top * inv).astype(BF16)
        out_ref[0, prompt_len:, cols] = (low * inv).astype(BF16)


def probs_of(queries, keys, prompt_len):
    slots, query_len, width = queries.shape
    key_len = keys.shape[1]
    heads = width // HEAD_SIZE
    return pl.pallas_call(
        functools.partial(probs_kernel, heads=heads, prompt_len=prompt_len),
        grid=(slots,),
        in_specs=[
            pl.BlockSpec((1, query_len, width), lambda r: (r, 0, 0)),
            pl.BlockSpec((1, key_len, HEAD_SIZE), lambda r: (r, 0, 0)),
        ],
        out_specs=pl.BlockSpec((1, key_len, heads * query_len), lambda r: (r, 0, 0)),
        out_shape=jax.ShapeDtypeStruct((slots, key_len, heads * query_len), BF16),
        compiler_params=pltpu.CompilerParams(vmem_limit_bytes=VMEM_LIMIT),
        cost_estimate=pl.CostEstimate(
            flops=4 * slots * heads * query_len * key_len * HEAD_SIZE,
            bytes_accessed=2 * slots * heads * query_len * key_len,
            transcendentals=slots * heads * query_len * key_len,
        ),
    )(queries, keys)


def blocks_of_a(a_pieces, order, shard_rows):
    out = []
    for at, dz in enumerate(order):
        parts = []
        for i, (dy, first, arr) in enumerate(a_pieces):
            source = at * shard_rows - first
            if 0 <= source < arr.shape[0]:
                parts.append((i, source, shard_rows, dy, 0))
        out.append((dz, tuple(parts)))
    return tuple(out)


def blocks_of_b(b_pieces, inner, shard_rows):
    out = {}
    for i, (dz, first, arr) in enumerate(b_pieces):
        parts = out.setdefault(dz, [])
        for k, dy in enumerate(inner):
            low, high = max(k * shard_rows, first), min((k + 1) * shard_rows, first + arr.shape[0])
            if low < high:
                parts.append((i, low - first, high - low, dy, low - k * shard_rows))
    return tuple((dz, tuple(parts)) for dz, parts in out.items())


def begin_loads(meta_ref, w_refs, scaled_ref, w_buf, scaled_buf, w_sems, s_sems, *, blocks, per_step, shard_rows, z_size):
    my_z, my_y = meta_ref[0], meta_ref[1]
    depth_z = Y_SIZE * shard_rows
    for at, (dz, parts) in enumerate(blocks):
        step, inside = at // per_step, at % per_step
        z = lax.rem(my_z + (dz + z_size), z_size)
        pltpu.make_async_copy(
            scaled_ref.at[:, :, pl.ds(pl.multiple_of(z * depth_z, HEAD_SIZE), depth_z)],
            scaled_buf.at[step, :, :, pl.ds(inside * depth_z, depth_z)],
            s_sems.at[step]).start()
        for i, source, rows, dy, first in parts:
            row = lax.rem(my_y + (dy + Y_SIZE), Y_SIZE) * shard_rows + (inside * depth_z + first)
            pltpu.make_async_copy(
                w_refs[i].at[pl.ds(source, rows), :],
                w_buf.at[step, pl.ds(pl.multiple_of(row, 16), rows), :], w_sems.at[step]).start()


def accumulate(acc, w_buf, scaled_buf, w_sems, s_sems):
    steps, slots, query_len, depth = scaled_buf.shape

    def multiply(step, carry):
        pltpu.make_async_copy(scaled_buf.at[step], scaled_buf.at[step], s_sems.at[step]).wait()
        pltpu.make_async_copy(w_buf.at[step], w_buf.at[step], w_sems.at[step]).wait()
        part = jnp.dot(scaled_buf[step].reshape(slots * query_len, depth), w_buf[step], preferred_element_type=F32)
        acc[...] += part.reshape(acc.shape)
        return carry

    lax.fori_loop(0, steps, multiply, 0)


def load_scratch(slots, query_len, cols, n_blocks, per_step, depth_z):
    steps = n_blocks // per_step
    return [
        pltpu.VMEM((steps, per_step * depth_z, cols), BF16),
        pltpu.VMEM((steps, slots, query_len, per_step * depth_z), BF16),
        pltpu.VMEM((slots, query_len, cols), F32),
        pltpu.SemaphoreType.DMA((steps,)),
        pltpu.SemaphoreType.DMA((steps,)),
    ]


def project_kernel(meta_ref, *refs, n_pieces, **loads):
    w_refs, (scaled_ref, out_ref, w_buf, scaled_buf, acc, w_sems, s_sems) = refs[:n_pieces], refs[n_pieces:]
    begin_loads(meta_ref, w_refs, scaled_ref, w_buf, scaled_buf, w_sems, s_sems, **loads)
    acc[...] = jnp.zeros_like(acc)
    accumulate(acc, w_buf, scaled_buf, w_sems, s_sems)
    out_ref[...] = acc[...].astype(out_ref.dtype)


def project(meta, pieces, blocks, per_step, scaled, dtype, shard_rows, z_size):
    slots, query_len, _ = scaled.shape
    cols = pieces[0].shape[1]
    depth_z = Y_SIZE * shard_rows
    anywhere = pl.BlockSpec(memory_space=pl.ANY)
    return pl.pallas_call(
        functools.partial(project_kernel, n_pieces=len(pieces), blocks=blocks, per_step=per_step,
                          shard_rows=shard_rows, z_size=z_size),
        grid_spec=pltpu.PrefetchScalarGridSpec(
            num_scalar_prefetch=1,
            grid=(1,),
            in_specs=[anywhere] * (len(pieces) + 1),
            out_specs=pl.BlockSpec((slots, query_len, cols), lambda i, m: (0, 0, 0)),
            scratch_shapes=load_scratch(slots, query_len, cols, len(blocks), per_step, depth_z),
        ),
        out_shape=jax.ShapeDtypeStruct((slots, query_len, cols), dtype),
        compiler_params=pltpu.CompilerParams(vmem_limit_bytes=VMEM_LIMIT),
        cost_estimate=pl.CostEstimate(
            flops=2 * slots * query_len * cols * depth_z * len(blocks),
            bytes_accessed=2 * depth_z * len(blocks) * (cols + slots * query_len),
            transcendentals=0,
        ),
    )(meta, *pieces, scaled)


def backward_kernel(meta_ref, *refs, n_pieces, heads, prompt_len, **loads):
    w_refs, refs = refs[:n_pieces], refs[n_pieces:]
    scaled_ref, probs_ref, part_ref, d_a_ref, q_ref, k_ref, v_ref, dq_ref, dk_ref, dv_ref, own_ref, *refs = refs
    sent_refs, refs = refs[:2 * SPREAD], refs[2 * SPREAD:]
    w_buf, scaled_buf, acc, w_sems, s_sems, probs_buf, do_buf, q_buf, ds_buf, sum_buf, p_sems = refs
    r = pl.program_id(0)
    slots, query_len = scaled_ref.shape[0], q_ref.shape[1]
    first_cols = d_a_ref.shape[2]

    @pl.when(r == 0)
    def _():
        begin_loads(meta_ref, w_refs, scaled_ref, w_buf, scaled_buf, w_sems, s_sems, **loads)
        for slot in range(slots):
            pltpu.make_async_copy(probs_ref.at[slot], probs_buf.at[slot], p_sems.at[slot]).start()
        sum_buf[...] = jnp.zeros_like(sum_buf)
        acc[...] = part_ref[...]
        accumulate(acc, w_buf, scaled_buf, w_sems, s_sems)

    pltpu.make_async_copy(probs_ref.at[r], probs_buf.at[r], p_sems.at[r]).wait()
    keys = k_ref[0]
    values = v_ref[0]
    for h in range(heads):
        rows = slice(h * query_len, (h + 1) * query_len)
        low, high = h * HEAD_SIZE, (h + 1) * HEAD_SIZE
        q_buf[rows, :] = q_ref[0, :, low:high]
        if high <= first_cols:
            d_out = d_a_ref[0, :, low:high]
        else:
            d_out = acc[r, :, low - first_cols:high - first_cols].astype(BF16)
        do_buf[rows, :] = d_out
        dprobs = lax.dot_general(values, d_out, (((1,), (1,)), ((), ())), preferred_element_type=F32)
        probs = probs_buf[r, :, rows].astype(F32)
        mean = jnp.sum(probs * dprobs, axis=0, keepdims=True)
        ds = (probs * (dprobs - mean)).astype(BF16)
        ds_buf[:, rows] = ds
        dq = lax.dot_general(ds, keys, (((0,), (0,)), ((), ())), preferred_element_type=F32) * head_scale
        dq_ref[0, :, low:high] = dq.astype(BF16)
    dk = jnp.dot(ds_buf[...], q_buf[...], preferred_element_type=F32) * head_scale
    dv = jnp.dot(probs_buf[r], do_buf[...], preferred_element_type=F32)
    dk_ref[0] = dk[prompt_len:].astype(BF16)
    dv_ref[0] = dv[prompt_len:].astype(BF16)
    offset = meta_ref[2 + r]
    for o in range(-SPREAD, SPREAD + 1):
        @pl.when(offset == o)
        def _():
            sum_buf[o + SPREAD, 0] += dk[:prompt_len]
            sum_buf[o + SPREAD, 1] += dv[:prompt_len]

    @pl.when(r == pl.num_programs(0) - 1)
    def _():
        own_ref[...] = sum_buf[SPREAD]
        for ref, o in zip(sent_refs, (-2, -1, 1, 2)):
            ref[...] = sum_buf[o + SPREAD].astype(BF16)


def backward_of(meta, pieces, blocks, per_step, scaled, probs, part, d_a, queries, keys, values, prompt_len,
                shard_rows, z_size):
    slots, query_len, width = queries.shape
    key_len = keys.shape[1]
    own_len = key_len - prompt_len
    heads = width // HEAD_SIZE
    cols = pieces[0].shape[1]
    depth_z = Y_SIZE * shard_rows
    by_slot = lambda *shape: pl.BlockSpec((1,) + shape, lambda r, m: (r, 0, 0))
    anywhere = pl.BlockSpec(memory_space=pl.ANY)
    whole = pl.BlockSpec((2, prompt_len, HEAD_SIZE), lambda r, m: (0, 0, 0))
    tile = lambda dtype: jax.ShapeDtypeStruct((2, prompt_len, HEAD_SIZE), dtype)
    return pl.pallas_call(
        functools.partial(backward_kernel, n_pieces=len(pieces), heads=heads, prompt_len=prompt_len, blocks=blocks,
                          per_step=per_step, shard_rows=shard_rows, z_size=z_size),
        grid_spec=pltpu.PrefetchScalarGridSpec(
            num_scalar_prefetch=1,
            grid=(slots,),
            in_specs=[anywhere] * (len(pieces) + 2) + [
                pl.BlockSpec((slots, query_len, cols), lambda r, m: (0, 0, 0)),
                by_slot(query_len, width - cols),
                by_slot(query_len, width),
                by_slot(key_len, HEAD_SIZE),
                by_slot(key_len, HEAD_SIZE),
            ],
            out_specs=[by_slot(query_len, width)] + [by_slot(own_len, HEAD_SIZE)] * 2 + [whole] * (2 * SPREAD + 1),
            scratch_shapes=load_scratch(slots, query_len, cols, len(blocks), per_step, depth_z) + [
                pltpu.VMEM((slots, key_len, heads * query_len), BF16),
                pltpu.VMEM((heads * query_len, HEAD_SIZE), BF16),
                pltpu.VMEM((heads * query_len, HEAD_SIZE), BF16),
                pltpu.VMEM((key_len, heads * query_len), BF16),
                pltpu.VMEM((2 * SPREAD + 1, 2, prompt_len, HEAD_SIZE), F32),
                pltpu.SemaphoreType.DMA((slots,)),
            ],
        ),
        out_shape=[jax.ShapeDtypeStruct((slots, query_len, width), BF16)]
        + [jax.ShapeDtypeStruct((slots, own_len, HEAD_SIZE), BF16)] * 2
        + [tile(F32)] + [tile(BF16)] * (2 * SPREAD),
        compiler_params=pltpu.CompilerParams(vmem_limit_bytes=VMEM_LIMIT),
        cost_estimate=pl.CostEstimate(
            flops=2 * slots * query_len * cols * depth_z * len(blocks) + 8 * slots * query_len * width * key_len,
            bytes_accessed=2 * depth_z * len(blocks) * (cols + slots * query_len),
            transcendentals=0,
        ),
    )(meta, *pieces, scaled, probs, part, d_a, queries, keys, values)


def after(values, *others):
    return lax.optimization_barrier((values, others))[0]


def on_device(queries, response_keys, response_values, out_grad, advantages, lengths, groups,
              prompt_keys, prompt_value_rows, w_out):
    slots, local_rows, width = out_grad.shape
    prompt_len = prompt_keys.shape[1]
    z_size = lax.axis_size("z")
    dp_count = z_size * lax.axis_size("y")
    my_z, my_y = lax.axis_index("z"), lax.axis_index("y")
    my_index = my_z * Y_SIZE + my_y
    tensor_index = lax.axis_index("x") * CORES + lax.axis_index("c")
    positions = tensor_index * local_rows + jnp.arange(local_rows, dtype=jnp.int32)
    live_mask = jnp.where(positions[None, :] < lengths[:, None], 1.0, 0.0).astype(F32)
    factor = advantages * live_mask * (loss_scale * RESPONSE_LENGTH / lengths.astype(F32))[:, None]
    scaled = (out_grad.astype(F32) * factor[:, :, None]).astype(BF16)
    half = w_out.shape[1] // 2
    w_a, w_b = w_out[:, :half], w_out[:, half:]
    shard_rows = w_out.shape[0]
    gathered = lax.all_gather(scaled, ("x", "c"), axis=1, tiled=True)
    z_parts = ring_gather(w_a, "z")
    b_inner = (0, -1, 1, 2)
    b_block = jnp.concatenate([w_b if dy == 0 else shift(w_b, "y", -dy) for dy in b_inner], 0)
    tile_pair = jnp.concatenate([prompt_keys[0], prompt_value_rows[0]], 0)
    tiles = {d: shift(tile_pair, ("z", "y"), -d) for d in (-2, -1, 1, 2)}
    a_block = jnp.concatenate([p[2] for p in z_parts], 0)
    a_block, tile_pair, tiles = lax.optimization_barrier((a_block, tile_pair, tiles))
    a_pieces = ring_gather(a_block, "y")

    raw_offsets = (groups - my_index) % dp_count
    offsets = jnp.where(raw_offsets > dp_count // 2, raw_offsets - dp_count, raw_offsets)
    tiles[0] = tile_pair

    meta = jnp.concatenate([jnp.stack([my_z, my_y]).astype(jnp.int32), offsets.astype(jnp.int32)])
    arrays = lambda pieces: [p[2] for p in pieces]

    received = jnp.zeros((slots,) + tile_pair.shape, BF16)
    for offset in range(-SPREAD, SPREAD + 1):
        received = jnp.where((offsets == offset)[:, None, None], tiles[offset][None], received)
    keys = jnp.concatenate([received[:, :prompt_len], response_keys], 1)
    values = jnp.concatenate([received[:, prompt_len:], response_values], 1)
    found = {"probs": probs_of(queries, keys, prompt_len)}

    def between(step, pieces, up, down):
        if step == 1:
            up, down, found["probs"] = lax.optimization_barrier((up, down, found["probs"]))
        elif step == 2:
            found["part"] = project(meta, arrays(pieces), blocks_of_b(pieces, b_inner, shard_rows), len(pieces),
                                    gathered, F32, shard_rows, z_size)
            up, down, found["part"] = lax.optimization_barrier((up, down, found["part"]))
        return up, down

    b_pieces = ring_gather(b_block, "z", between)
    order = [rel for rel, first, _ in z_parts if first == 0]
    late = b_pieces[3:]
    d_a = project(meta, arrays(a_pieces), blocks_of_a(a_pieces, order, shard_rows), 2, gathered, BF16, shard_rows, z_size)
    query_grad, key_grad, value_grad, own, *sent = backward_of(
        meta, arrays(late), blocks_of_b(late, b_inner, shard_rows), 1, gathered, found["probs"], found["part"], d_a,
        queries, keys, values, prompt_len, shard_rows, z_size)
    summed = own
    for offset, tile in zip((-2, -1, 1, 2), sent):
        summed = summed + shift(tile, ("z", "y"), offset).astype(F32)
    return query_grad, key_grad, value_grad, summed[:1], summed[1:]


def solution(mesh):
    dp_count, tensor_count = mesh.devices.shape
    fine = Mesh(
        mesh.devices.reshape(dp_count // Y_SIZE, Y_SIZE, tensor_count // CORES, CORES),
        ("z", "y", "x", "c"),
    )
    dp, tensor = ("z", "y"), ("x", "c")
    in_specs = (
        P(dp, None, tensor),
        P(dp, None, tensor),
        P(dp, None, tensor),
        P(dp, tensor, None),
        P(dp, tensor),
        P(dp),
        P(dp),
        P(dp, None, tensor),
        P(dp, None, tensor),
        P(dp, tensor),
    )
    out_specs = (P(dp, None, tensor),) * 5
    return jax.shard_map(on_device, mesh=fine, in_specs=in_specs, out_specs=out_specs, check_vma=False)
```

time: 281 us -> 161 us (0.57)
  waiting for transfers between devices: 155 us -> 29.7 us
  matrix products: 49 us -> 0 us
  Pallas kernels: 0 us -> 43.6 us
  starting transfers between devices: 17 us -> 55.5 us
  local copies, waits for them, and re-layouts: 31.8 us -> 10.6 us
  other arithmetic: 12.2 us -> 7.33 us
    all_gather x2 -> x1, waiting for transfers between devices: 141 us -> 0.01 us  [on_device(): gathered = lax.all_gather(scaled, ('x', 'c'), axis=1, tiled=True)]
    dot_general x16 -> x0, matrix products: 49 us -> none  [the longest x1 14.2 us: on_device(): jnp.dot(flat_rows, lax.all_gather(w_out, 'dp', axis=0, tiled=True), prefe...]
    pallas_call x0 -> x4, Pallas kernels: none -> 43.6 us  [the longest x1 20 us: backward_of(): pl.pallas_call(functools.partial(backward_kernel, n_pieces=len(pieces), h...]
    ppermute x8 -> x31, starting transfers between devices: 16.9 us -> 55.5 us  [shift(): return lax.ppermute(block, axis, route)]
    ppermute x8 -> x31, waiting for transfers between devices: 13.5 us -> 29.7 us  [shift(): return lax.ppermute(block, axis, route)]
    dynamic_slice x18 -> x0, local copies, waits for them, and re-layouts: 8.35 us -> none  [on_device(): lax.map(per_slot, (queries, response_keys, response_values, taken_keys, t...]
    while x14 -> x0, local copies, waits for them, and re-layouts: 7.36 us -> none
    dynamic_update_slice x6 -> x0, local copies, waits for them, and re-layouts: 6.24 us -> none  [on_device(): lax.map(per_slot, (queries, response_keys, response_values, taken_keys, t...]
  transfers between devices with their start and end apart: 10 -> 32, of which waited for: 9 -> 10; matrix products, arithmetic and copies ran while one was open for 2% -> 7% of each run, Pallas kernels for 0% -> 15%
where the time goes in v1:
time: 161 us
  starting transfers between devices  55.5 us (34%)
  Pallas kernels  43.6 us (27%)
  waiting for transfers between devices  29.7 us (18%)
  between operations  14.4 us (9%)
  local copies, waits for them, and re-layouts  10.6 us (7%)
  other arithmetic  7.33 us (5%)
    ppermute x31, starting transfers between devices, shift(): return lax.ppermute(block, axis, route)  55.5 us
    ppermute x31, waiting for transfers between devices, shift(): return lax.ppermute(block, axis, route)  29.7 us
    pallas_call x1, Pallas kernels, backward_of(): pl.pallas_call(functools.partial(backward_kernel, n_pieces=len(pieces), h...  20 us
    pallas_call x2, Pallas kernels, project(): pl.pallas_call(functools.partial(project_kernel, n_pieces=len(pieces), bl...  15.4 us
    pallas_call x1, Pallas kernels, probs_of(): pl.pallas_call(functools.partial(probs_kernel, heads=heads, prompt_len=pr...  8.17 us
    unnamed x39, local copies, waits for them, and re-layouts  6.19 us
  transfers between devices with their start and end apart: 32, of which 10 were waited for; matrix products, arithmetic and copies ran while one was open for 7% of the time, Pallas kernels for 15%

profile of v1, /device:TPU:2, one launch (start us, length us, event | category | flops | bytes accessed | tf_op | source)
XLA Modules:
  0.0 161.1 jit_solution(235506530547750126)
XLA Ops:
  7.9 0.8 multiply_multiply_fusion
  8.7 2.5 %multiply_convert_fusion = bf16[3,32,5120]{2,1,0:T(8,128)(2,1)} fusion(bf16[3,32,5120]{2,1,0:T(8,128)(2,1)} %param.13, f32[3,32]{1,0:T(4,128)S(1)} %multiply_multiply_fusion), kind=kLoop, calls=%fused_computation | loop fusion | flops 1474560 | bytes 1966464 | tf_op jit(solution)/shard_map/convert_element_type | solution.py:307
  11.1 0.7 fusion.2
  11.9 5.9 %collective-permute-start.6 = (bf16[160,512]{1,0:T(8,128)(2,1)S(1)}, bf16[160,512]{1,0:T(8,128)(2,1)S(1)}, u32[]{:S(2)}, u32[]{:S(2)}) collective-permute-start(bf16[160,512]{1,0:T(8,128)(2,1)S(1)} %get-tuple-element.61), channel_id=1, source_target_pairs={{0,224},{32,0},{64,32},{96,64},{128,96},{160,128},{192,160},{224,1... | collective-permute-start | bytes 491528 | tf_op jit(solution)/shard_map/ppermute | solution.py:28
  17.7 3.2 %collective-permute-start.2 = (bf16[160,512]{1,0:T(8,128)(2,1)S(1)}, bf16[160,512]{1,0:T(8,128)(2,1)S(1)}, u32[]{:S(2)}, u32[]{:S(2)}) collective-permute-start(bf16[160,512]{1,0:T(8,128)(2,1)S(1)} %get-tuple-element.63), channel_id=1, source_target_pairs={{0,16},{8,24},{16,0},{24,8},{1,17},{9,25},{17,1},{25,9},{2,18},{10... | collective-permute-start | bytes 491528 | tf_op jit(solution)/shard_map/ppermute | solution.py:28
  20.9 1.1 collective-permute-start.1
  22.0 1.0 collective-permute-start
  23.0 3.3 %collective-permute-start.8 = (bf16[160,512]{1,0:T(8,128)(2,1)S(1)}, bf16[160,512]{1,0:T(8,128)(2,1)S(1)}, u32[]{:S(2)}, u32[]{:S(2)}) collective-permute-start(bf16[160,512]{1,0:T(8,128)(2,1)S(1)} %collective-permute-done.6), channel_id=1, source_target_pairs={{0,224},{32,0},{64,32},{96,64},{128,96},{160,128},{192,160},{224,1... | collective-permute-start | bytes 491528 | tf_op jit(solution)/shard_map/ppermute | solution.py:28
  26.3 0.7 constant_dynamic-update-slice_fusion.7
  27.0 0.7 constant_dynamic-update-slice_fusion.6
  27.7 4.5 %collective-permute-start.16 = (bf16[512,128]{1,0:T(8,128)(2,1)S(1)}, bf16[512,128]{1,0:T(8,128)(2,1)S(1)}, u32[]{:S(2)}, u32[]{:S(2)}) collective-permute-start(bf16[512,128]{1,0:T(8,128)(2,1)S(1)} %pad_maximum_fusion.3), channel_id=1, source_target_pairs={{0,240},{8,248},{16,0},{24,8},{32,16},{40,24},{48,32},{56,40},{64,... | collective-permute-start | bytes 393224 | tf_op jit(solution)/shard_map/ppermute | solution.py:28
  32.2 1.6 collective-permute-start.15
  34.4 2.0 %collective-permute-start.9 = (bf16[160,512]{1,0:T(8,128)(2,1)S(1)}, bf16[160,512]{1,0:T(8,128)(2,1)S(1)}, u32[]{:S(2)}, u32[]{:S(2)}) collective-permute-start(bf16[160,512]{1,0:T(8,128)(2,1)S(1)} %collective-permute-done.7), channel_id=1, source_target_pairs={{0,32},{32,64},{64,96},{96,128},{128,160},{160,192},{192,224},{224... | collective-permute-start | bytes 491528 | tf_op jit(solution)/shard_map/ppermute | solution.py:28
  36.4 0.7 constant_dynamic-update-slice_fusion.5
  37.1 0.7 constant_dynamic-update-slice_fusion.4
  37.8 3.2 %collective-permute-done.10 = bf16[160,512]{1,0:T(8,128)(2,1)S(1)} collective-permute-done((bf16[160,512]{1,0:T(8,128)(2,1)S(1)}, bf16[160,512]{1,0:T(8,128)(2,1)S(1)}, u32[]{:S(2)}, u32[]{:S(2)}) %collective-permute-start.10) | collective-permute-done | bytes 163872 | tf_op jit(solution)/shard_map/ppermute | solution.py:28
  41.1 0.7 collective-permute-start.11
  41.8 0.7 constant_dynamic-update-slice_fusion.3
  42.4 0.7 constant_dynamic-update-slice_fusion.2
  43.1 4.1 %collective-permute-done.11 = bf16[80,512]{1,0:T(8,128)(2,1)S(1)} collective-permute-done((bf16[80,512]{1,0:T(8,128)(2,1)S(1)}, bf16[80,512]{1,0:T(8,128)(2,1)S(1)}, u32[]{:S(2)}, u32[]{:S(2)}) %collective-permute-start.11) | collective-permute-done | bytes 81952 | tf_op jit(solution)/shard_map/ppermute | solution.py:28
  47.3 2.0 %collective-permute-start.12 = (bf16[80,512]{1,0:T(8,128)(2,1)S(1)}, bf16[80,512]{1,0:T(8,128)(2,1)S(1)}, u32[]{:S(2)}, u32[]{:S(2)}) collective-permute-start(bf16[80,512]{1,0:T(8,128)(2,1)S(1)} %slice.49), channel_id=1, source_target_pairs={{0,224},{32,0},{64,32},{96,64},{128,96},{160,128},{192,160},{224,1... | collective-permute-start | bytes 245768 | tf_op jit(solution)/shard_map/ppermute | solution.py:28
  49.9 1.9 %collective-permute-done.12 = bf16[80,512]{1,0:T(8,128)(2,1)S(1)} collective-permute-done((bf16[80,512]{1,0:T(8,128)(2,1)S(1)}, bf16[80,512]{1,0:T(8,128)(2,1)S(1)}, u32[]{:S(2)}, u32[]{:S(2)}) %collective-permute-start.12) | collective-permute-done | bytes 81952 | tf_op jit(solution)/shard_map/ppermute | solution.py:28
  51.8 3.1 %collective-permute-start.4 = (bf16[640,512]{1,0:T(8,128)(2,1)S(1)}, bf16[640,512]{1,0:T(8,128)(2,1)S(1)}, u32[]{:S(2)}, u32[]{:S(2)}) collective-permute-start(bf16[640,512]{1,0:T(8,128)(2,1)S(1)} %pad_maximum_fusion.refs_0_), channel_id=1, source_target_pairs={{0,224},{32,0},{64,32},{96,64},{128,96},{160,128},{192,160},{224,1... | collective-permute-start | bytes 1966088 | tf_op jit(solution)/shard_map/ppermute | solution.py:28
  55.6 5.5 %collective-permute-start.24 = (bf16[1280,512]{1,0:T(8,128)(2,1)}, bf16[1280,512]{1,0:T(8,128)(2,1)}, u32[]{:S(2)}, u32[]{:S(2)}) collective-permute-start(bf16[1280,512]{1,0:T(8,128)(2,1)} %constant_dynamic-update-slice_fusion.refs_0_), channel_id=1, source_target_pairs={{0,24},{8,0},{16,8},{24,16},{1,25},{9,1},{17,9},{25,17},{2,26},{10... | collective-permute-start | bytes 3932168 | tf_op jit(solution)/shard_map/ppermute | solution.py:28
  61.3 0.8 pad_maximum_fusion.1.k_ref.refs_11_
  62.1 8.2 %shard_map.137.refs_7_ = bf16[3,512,2048]{2,1,0:T(8,128)(2,1)} custom-call(bf16[3,256,1024]{2,1,0:T(8,128)(2,1)} %refs_10_.1, bf16[3,512,128]{2,1,0:T(8,128)(2,1)} %pad_maximum_fusion.1.k_ref.refs_11_), custom_call_target="tpu_custom_call" | custom-call | flops 1610612736 | bytes 6291456 | tf_op jit(solution)/shard_map/pallas_call | solution.py:74
  70.5 3.2 %collective-permute-start.18 = (bf16[640,512]{1,0:T(8,128)(2,1)S(1)}, bf16[640,512]{1,0:T(8,128)(2,1)S(1)}, u32[]{:S(2)}, u32[]{:S(2)}) collective-permute-start(bf16[640,512]{1,0:T(8,128)(2,1)S(1)} %collective-permute-done.4.refs_2_), channel_id=1, source_target_pairs={{0,224},{32,0},{64,32},{96,64},{128,96},{160,128},{192,160},{224,1... | collective-permute-start | bytes 1966088 | tf_op jit(solution)/shard_map/ppermute | solution.py:28
  74.4 6.1 %shard_map.138.refs_8_ = f32[3,256,512]{2,1,0:T(8,128)} custom-call(s32[5]{0:T(128)} %pad_add_fusion.meta_ref, bf16[640,512]{1,0:T(8,128)(2,1)} %copy-done, bf16[640,512]{1,0:T(8,128)(2,1)} %copy-done.6, bf16[640,512]{1,0:T(8,128)(2,1)} %copy-done.5, bf16[3,256,5120]{2,1,0:T(8,128)(2,1)} %all-gather.2.cloned.1.call-done.refs_3_.refs_5_.refs_6_), custom_call_target="tpu_custom_call" | custom-call | flops 1509949440 | bytes 4915200 | tf_op jit(solution)/shard_map/pallas_call | solution.py:169
  80.5 4.7 %collective-permute-done.17.refs_0_ = bf16[640,512]{1,0:T(8,128)(2,1)S(1)} collective-permute-done((bf16[640,512]{1,0:T(8,128)(2,1)S(1)}, bf16[640,512]{1,0:T(8,128)(2,1)S(1)}, u32[]{:S(2)}, u32[]{:S(2)}) %collective-permute-start.17) | collective-permute-done | bytes 655392 | tf_op jit(solution)/shard_map/ppermute | solution.py:28
  85.3 3.2 %collective-permute-start.20 = (bf16[640,512]{1,0:T(8,128)(2,1)S(1)}, bf16[640,512]{1,0:T(8,128)(2,1)S(1)}, u32[]{:S(2)}, u32[]{:S(2)}) collective-permute-start(bf16[640,512]{1,0:T(8,128)(2,1)S(1)} %collective-permute-done.18.refs_1_), channel_id=1, source_target_pairs={{0,224},{32,0},{64,32},{96,64},{128,96},{160,128},{192,160},{224,1... | collective-permute-start | bytes 1966088 | tf_op jit(solution)/shard_map/ppermute | solution.py:28
  88.5 1.1 slice.54
  89.6 1.1 slice.53
  90.8 2.9 %collective-permute-start.25 = (bf16[640,512]{1,0:T(8,128)(2,1)S(1)}, bf16[640,512]{1,0:T(8,128)(2,1)S(1)}, u32[]{:S(2)}, u32[]{:S(2)}) collective-permute-start(bf16[640,512]{1,0:T(8,128)(2,1)S(1)} %slice.53), channel_id=1, source_target_pairs={{0,8},{8,16},{16,24},{24,0},{1,9},{9,17},{17,25},{25,1},{2,10},{10... | collective-permute-start | bytes 1966088 | tf_op jit(solution)/shard_map/ppermute | solution.py:28
  93.7 0.7 collective-permute-start.26
  94.4 0.8 pad_maximum_fusion.2.refs_12_
  95.2 4.8 %collective-permute-done.19.refs_2_ = bf16[640,512]{1,0:T(8,128)(2,1)S(1)} collective-permute-done((bf16[640,512]{1,0:T(8,128)(2,1)S(1)}, bf16[640,512]{1,0:T(8,128)(2,1)S(1)}, u32[]{:S(2)}, u32[]{:S(2)}) %collective-permute-start.19) | collective-permute-done | bytes 655392 | tf_op jit(solution)/shard_map/ppermute | solution.py:28
  100.2 3.2 %collective-permute-start.22 = (bf16[320,512]{1,0:T(8,128)(2,1)S(1)}, bf16[320,512]{1,0:T(8,128)(2,1)S(1)}, u32[]{:S(2)}, u32[]{:S(2)}) collective-permute-start(bf16[320,512]{1,0:T(8,128)(2,1)S(1)} %slice.52), channel_id=1, source_target_pairs={{0,224},{32,0},{64,32},{96,64},{128,96},{160,128},{192,160},{224,1... | collective-permute-start | bytes 983048 | tf_op jit(solution)/shard_map/ppermute | solution.py:28
  103.4 1.0 collective-permute-done.26.refs_4_
  104.4 9.3 %shard_map.139.refs_9_ = bf16[3,256,512]{2,1,0:T(8,128)(2,1)} custom-call(s32[5]{0:T(128)} %pad_add_fusion.meta_ref, bf16[1280,512]{1,0:T(8,128)(2,1)} %constant_dynamic-update-slice_fusion.refs_0_, bf16[1280,512]{1,0:T(8,128)(2,1)} %collective-permute-done.23.refs_1_, bf16[1280,512]{1,0:T(8,128)(2,1)} %collective-permute-done.24.refs_2_, ...), custom_call_target="tpu_custom_call" | custom-call | flops 4026531840 | bytes 13107200 | tf_op jit(solution)/shard_map/pallas_call | solution.py:169
  113.8 0.7 copy-done.8
  114.5 0.7 copy-done.9
  115.2 20.0 %shard_map.140 = (bf16[3,256,1024]{2,1,0:T(8,128)(2,1)}, bf16[3,256,128]{2,1,0:T(8,128)(2,1)}, bf16[3,256,128]{2,1,0:T(8,128)(2,1)}, f32[2,256,128]{2,1,0:T(8,12...) custom-call(s32[5]{0:T(128)} %pad_add_fusion.meta_ref, ...), custom_call_target="tpu_custom_call" | custom-call | flops 5737807872 | bytes 8192000 | tf_op jit(solution)/shard_map/pallas_call | solution.py:256
  135.2 4.7 %collective-permute-start.27 = (bf16[2,256,128]{2,1,0:T(8,128)(2,1)}, bf16[2,256,128]{2,1,0:T(8,128)(2,1)S(1)}, u32[]{:S(2)}, u32[]{:S(2)}) collective-permute-start(bf16[2,256,128]{2,1,0:T(8,128)(2,1)} %get-tuple-element.53), channel_id=1, source_target_pairs={{0,240},{8,248},{16,0},{24,8},{32,16},{40,24},{48,32},{56,40},{64,... | collective-permute-start | bytes 393224 | tf_op jit(solution)/shard_map/ppermute | solution.py:28
  139.9 2.7 %collective-permute-start.28 = (bf16[2,256,128]{2,1,0:T(8,128)(2,1)}, bf16[2,256,128]{2,1,0:T(8,128)(2,1)S(1)}, u32[]{:S(2)}, u32[]{:S(2)}) collective-permute-start(bf16[2,256,128]{2,1,0:T(8,128)(2,1)} %get-tuple-element.54), channel_id=1, source_target_pairs={{0,248},{8,0},{16,8},{24,16},{32,24},{40,32},{48,40},{56,48},{64,5... | collective-permute-start | bytes 393224 | tf_op jit(solution)/shard_map/ppermute | solution.py:28
  142.9 2.5 %collective-permute-done.28 = bf16[2,256,128]{2,1,0:T(8,128)(2,1)S(1)} collective-permute-done((bf16[2,256,128]{2,1,0:T(8,128)(2,1)}, bf16[2,256,128]{2,1,0:T(8,128)(2,1)S(1)}, u32[]{:S(2)}, u32[]{:S(2)}) %collective-permute-start.28) | collective-permute-done | bytes 131104 | tf_op jit(solution)/shard_map/ppermute | solution.py:28
  145.4 6.7 %collective-permute-done.29 = bf16[2,256,128]{2,1,0:T(8,128)(2,1)S(1)} collective-permute-done((bf16[2,256,128]{2,1,0:T(8,128)(2,1)}, bf16[2,256,128]{2,1,0:T(8,128)(2,1)S(1)}, u32[]{:S(2)}, u32[]{:S(2)}) %collective-permute-start.29) | collective-permute-done | bytes 131104 | tf_op jit(solution)/shard_map/ppermute | solution.py:28
  152.5 1.0 convert_add_fusion
  153.5 0.7 fusion.3
  (83 shorter events, 4.6 us)
Async XLA Ops:
  7.2 67.2 %all-gather.2.cloned.1.call-start = ((), (), s32[]{:S(2)}) async-start(), calls=%async_computation | async-start | bytes 8847360 | tf_op jit(solution)/shard_map/all_gather | solution.py:311
  8.6 2.5 %copy-start.7 = (bf16[160,1024]{1,0:T(8,128)(2,1)S(1)}, bf16[160,1024]{1,0:T(8,128)(2,1)}, u32[]{:S(2)}) copy-start(bf16[160,1024]{1,0:T(8,128)(2,1)} %param.19) | copy-start | bytes 983044
  11.1 11.8 %copy-start.14 = (s32[3]{0:T(128)S(1)}, s32[3]{0:T(128)}, u32[]{:S(2)}) copy-start(s32[3]{0:T(128)} %param.16) | copy-start | bytes 40
  11.1 11.9 %copy-start.12 = (bf16[1,256,128]{2,1,0:T(8,128)(2,1)S(1)}, bf16[1,256,128]{2,1,0:T(8,128)(2,1)}, u32[]{:S(2)}) copy-start(bf16[1,256,128]{2,1,0:T(8,128)(2,1)} %param.18) | copy-start | bytes 196612
  11.1 11.9 %copy-start.13 = (bf16[1,256,128]{2,1,0:T(8,128)(2,1)S(1)}, bf16[1,256,128]{2,1,0:T(8,128)(2,1)}, u32[]{:S(2)}) copy-start(bf16[1,256,128]{2,1,0:T(8,128)(2,1)} %param.17) | copy-start | bytes 196612
  11.9 11.2 %collective-permute-start.6 = (bf16[160,512]{1,0:T(8,128)(2,1)S(1)}, bf16[160,512]{1,0:T(8,128)(2,1)S(1)}, u32[]{:S(2)}, u32[]{:S(2)}) collective-permute-start(bf16[160,512]{1,0:T(8,128)(2,1)S(1)} %get-tuple-element.61), channel_id=1, source_target_pairs={{0,224},{32,0},{64,32},{96,64},{128,96},{160,128},{192,160},{224,1... | collective-permute-start | bytes 491528 | tf_op jit(solution)/shard_map/ppermute | solution.py:28
  17.7 8.6 %collective-permute-start.5 = (bf16[160,512]{1,0:T(8,128)(2,1)S(1)}, bf16[160,512]{1,0:T(8,128)(2,1)S(1)}, u32[]{:S(2)}, u32[]{:S(2)}) collective-permute-start(bf16[160,512]{1,0:T(8,128)(2,1)S(1)} %get-tuple-element.61), channel_id=1, source_target_pairs={{0,32},{32,64},{64,96},{96,128},{128,160},{160,192},{192,224},{224... | collective-permute-start | bytes 491528 | tf_op jit(solution)/shard_map/ppermute | solution.py:28
  17.7 10.0 %collective-permute-start.2 = (bf16[160,512]{1,0:T(8,128)(2,1)S(1)}, bf16[160,512]{1,0:T(8,128)(2,1)S(1)}, u32[]{:S(2)}, u32[]{:S(2)}) collective-permute-start(bf16[160,512]{1,0:T(8,128)(2,1)S(1)} %get-tuple-element.63), channel_id=1, source_target_pairs={{0,16},{8,24},{16,0},{24,8},{1,17},{9,25},{17,1},{25,9},{2,18},{10... | collective-permute-start | bytes 491528 | tf_op jit(solution)/shard_map/ppermute | solution.py:28
  20.9 11.3 %collective-permute-start.1 = (bf16[160,512]{1,0:T(8,128)(2,1)S(1)}, bf16[160,512]{1,0:T(8,128)(2,1)S(1)}, u32[]{:S(2)}, u32[]{:S(2)}) collective-permute-start(bf16[160,512]{1,0:T(8,128)(2,1)S(1)} %get-tuple-element.63), channel_id=1, source_target_pairs={{0,24},{8,0},{16,8},{24,16},{1,25},{9,1},{17,9},{25,17},{2,26},{10... | collective-permute-start | bytes 491528 | tf_op jit(solution)/shard_map/ppermute | solution.py:28
  22.0 11.8 %collective-permute-start = (bf16[160,512]{1,0:T(8,128)(2,1)S(1)}, bf16[160,512]{1,0:T(8,128)(2,1)S(1)}, u32[]{:S(2)}, u32[]{:S(2)}) collective-permute-start(bf16[160,512]{1,0:T(8,128)(2,1)S(1)} %get-tuple-element.63), channel_id=1, source_target_pairs={{0,8},{8,16},{16,24},{24,0},{1,9},{9,17},{17,25},{25,1},{2,10},{10... | collective-permute-start | bytes 491528 | tf_op jit(solution)/shard_map/ppermute | solution.py:28
  23.0 11.3 %collective-permute-start.8 = (bf16[160,512]{1,0:T(8,128)(2,1)S(1)}, bf16[160,512]{1,0:T(8,128)(2,1)S(1)}, u32[]{:S(2)}, u32[]{:S(2)}) collective-permute-start(bf16[160,512]{1,0:T(8,128)(2,1)S(1)} %collective-permute-done.6), channel_id=1, source_target_pairs={{0,224},{32,0},{64,32},{96,64},{128,96},{160,128},{192,160},{224,1... | collective-permute-start | bytes 491528 | tf_op jit(solution)/shard_map/ppermute | solution.py:28
  26.3 8.1 %collective-permute-start.7 = (bf16[160,512]{1,0:T(8,128)(2,1)S(1)}, bf16[160,512]{1,0:T(8,128)(2,1)S(1)}, u32[]{:S(2)}, u32[]{:S(2)}) collective-permute-start(bf16[160,512]{1,0:T(8,128)(2,1)S(1)} %collective-permute-done.5), channel_id=1, source_target_pairs={{0,32},{32,64},{64,96},{96,128},{128,160},{160,192},{192,224},{224... | collective-permute-start | bytes 491528 | tf_op jit(solution)/shard_map/ppermute | solution.py:28
  27.7 27.9 %collective-permute-start.16 = (bf16[512,128]{1,0:T(8,128)(2,1)S(1)}, bf16[512,128]{1,0:T(8,128)(2,1)S(1)}, u32[]{:S(2)}, u32[]{:S(2)}) collective-permute-start(bf16[512,128]{1,0:T(8,128)(2,1)S(1)} %pad_maximum_fusion.3), channel_id=1, source_target_pairs={{0,240},{8,248},{16,0},{24,8},{32,16},{40,24},{48,32},{56,40},{64,... | collective-permute-start | bytes 393224 | tf_op jit(solution)/shard_map/ppermute | solution.py:28
  32.2 23.4 %collective-permute-start.15 = (bf16[512,128]{1,0:T(8,128)(2,1)S(1)}, bf16[512,128]{1,0:T(8,128)(2,1)S(1)}, u32[]{:S(2)}, u32[]{:S(2)}) collective-permute-start(bf16[512,128]{1,0:T(8,128)(2,1)S(1)} %pad_maximum_fusion.3), channel_id=1, source_target_pairs={{0,248},{8,0},{16,8},{24,16},{32,24},{40,32},{48,40},{56,48},{64,5... | collective-permute-start | bytes 393224 | tf_op jit(solution)/shard_map/ppermute | solution.py:28
  33.8 21.8 %collective-permute-start.14 = (bf16[512,128]{1,0:T(8,128)(2,1)S(1)}, bf16[512,128]{1,0:T(8,128)(2,1)S(1)}, u32[]{:S(2)}, u32[]{:S(2)}) collective-permute-start(bf16[512,128]{1,0:T(8,128)(2,1)S(1)} %pad_maximum_fusion.3), channel_id=1, source_target_pairs={{0,8},{8,16},{16,24},{24,32},{32,40},{40,48},{48,56},{56,64},{64,7... | collective-permute-start | bytes 393224 | tf_op jit(solution)/shard_map/ppermute | solution.py:28
  34.3 26.9 %copy-start = (bf16[640,512]{1,0:T(8,128)(2,1)}, bf16[640,512]{1,0:T(8,128)(2,1)S(1)}, u32[]{:S(2)}) copy-start(bf16[640,512]{1,0:T(8,128)(2,1)S(1)} %pad_maximum_fusion.refs_0_) | copy-start | bytes 1966084
  34.3 6.7 %collective-permute-start.10 = (bf16[160,512]{1,0:T(8,128)(2,1)S(1)}, bf16[160,512]{1,0:T(8,128)(2,1)S(1)}, u32[]{:S(2)}, u32[]{:S(2)}) collective-permute-start(bf16[160,512]{1,0:T(8,128)(2,1)S(1)} %collective-permute-done.8), channel_id=1, source_target_pairs={{0,224},{32,0},{64,32},{96,64},{128,96},{160,128},{192,160},{224,1... | collective-permute-start | bytes 491528 | tf_op jit(solution)/shard_map/ppermute | solution.py:28
  34.4 6.6 %collective-permute-start.9 = (bf16[160,512]{1,0:T(8,128)(2,1)S(1)}, bf16[160,512]{1,0:T(8,128)(2,1)S(1)}, u32[]{:S(2)}, u32[]{:S(2)}) collective-permute-start(bf16[160,512]{1,0:T(8,128)(2,1)S(1)} %collective-permute-done.7), channel_id=1, source_target_pairs={{0,32},{32,64},{64,96},{96,128},{128,160},{160,192},{192,224},{224... | collective-permute-start | bytes 491528 | tf_op jit(solution)/shard_map/ppermute | solution.py:28
  41.0 14.6 %collective-permute-start.13 = (bf16[512,128]{1,0:T(8,128)(2,1)S(1)}, bf16[512,128]{1,0:T(8,128)(2,1)S(1)}, u32[]{:S(2)}, u32[]{:S(2)}) collective-permute-start(bf16[512,128]{1,0:T(8,128)(2,1)S(1)} %pad_maximum_fusion.3), channel_id=1, source_target_pairs={{0,16},{8,24},{16,32},{24,40},{32,48},{40,56},{48,64},{56,72},{64,... | collective-permute-start | bytes 393224 | tf_op jit(solution)/shard_map/ppermute | solution.py:28
  41.1 6.2 %collective-permute-start.11 = (bf16[80,512]{1,0:T(8,128)(2,1)S(1)}, bf16[80,512]{1,0:T(8,128)(2,1)S(1)}, u32[]{:S(2)}, u32[]{:S(2)}) collective-permute-start(bf16[80,512]{1,0:T(8,128)(2,1)S(1)} %slice.48), channel_id=1, source_target_pairs={{0,32},{32,64},{64,96},{96,128},{128,160},{160,192},{192,224},{224... | collective-permute-start | bytes 245768 | tf_op jit(solution)/shard_map/ppermute | solution.py:28
  42.4 18.9 %copy-start.10 = (bf16[3,256,128]{2,1,0:T(8,128)(2,1)S(1)}, bf16[3,256,128]{2,1,0:T(8,128)(2,1)}, u32[]{:S(2)}) copy-start(bf16[3,256,128]{2,1,0:T(8,128)(2,1)} %param.11) | copy-start | bytes 589828
  47.3 4.6 %collective-permute-start.12 = (bf16[80,512]{1,0:T(8,128)(2,1)S(1)}, bf16[80,512]{1,0:T(8,128)(2,1)S(1)}, u32[]{:S(2)}, u32[]{:S(2)}) collective-permute-start(bf16[80,512]{1,0:T(8,128)(2,1)S(1)} %slice.49), channel_id=1, source_target_pairs={{0,224},{32,0},{64,32},{96,64},{128,96},{160,128},{192,160},{224,1... | collective-permute-start | bytes 245768 | tf_op jit(solution)/shard_map/ppermute | solution.py:28
  51.8 18.4 %collective-permute-start.4 = (bf16[640,512]{1,0:T(8,128)(2,1)S(1)}, bf16[640,512]{1,0:T(8,128)(2,1)S(1)}, u32[]{:S(2)}, u32[]{:S(2)}) collective-permute-start(bf16[640,512]{1,0:T(8,128)(2,1)S(1)} %pad_maximum_fusion.refs_0_), channel_id=1, source_target_pairs={{0,224},{32,0},{64,32},{96,64},{128,96},{160,128},{192,160},{224,1... | collective-permute-start | bytes 1966088 | tf_op jit(solution)/shard_map/ppermute | solution.py:28
  55.6 14.9 %collective-permute-start.3 = (bf16[640,512]{1,0:T(8,128)(2,1)S(1)}, bf16[640,512]{1,0:T(8,128)(2,1)S(1)}, u32[]{:S(2)}, u32[]{:S(2)}) collective-permute-start(bf16[640,512]{1,0:T(8,128)(2,1)S(1)} %pad_maximum_fusion.refs_0_), channel_id=1, source_target_pairs={{0,32},{32,64},{64,96},{96,128},{128,160},{160,192},{192,224},{224... | collective-permute-start | bytes 1966088 | tf_op jit(solution)/shard_map/ppermute | solution.py:28
  55.6 32.9 %collective-permute-start.24 = (bf16[1280,512]{1,0:T(8,128)(2,1)}, bf16[1280,512]{1,0:T(8,128)(2,1)}, u32[]{:S(2)}, u32[]{:S(2)}) collective-permute-start(bf16[1280,512]{1,0:T(8,128)(2,1)} %constant_dynamic-update-slice_fusion.refs_0_), channel_id=1, source_target_pairs={{0,24},{8,0},{16,8},{24,16},{1,25},{9,1},{17,9},{25,17},{2,26},{10... | collective-permute-start | bytes 3932168 | tf_op jit(solution)/shard_map/ppermute | solution.py:28
  61.1 28.6 %collective-permute-start.23 = (bf16[1280,512]{1,0:T(8,128)(2,1)}, bf16[1280,512]{1,0:T(8,128)(2,1)}, u32[]{:S(2)}, u32[]{:S(2)}) collective-permute-start(bf16[1280,512]{1,0:T(8,128)(2,1)} %constant_dynamic-update-slice_fusion.refs_0_), channel_id=1, source_target_pairs={{0,8},{8,16},{16,24},{24,0},{1,9},{9,17},{17,25},{25,1},{2,10},{10... | collective-permute-start | bytes 3932168 | tf_op jit(solution)/shard_map/ppermute | solution.py:28
  70.3 4.1 %copy-start.5 = (bf16[640,512]{1,0:T(8,128)(2,1)}, bf16[640,512]{1,0:T(8,128)(2,1)S(1)}, u32[]{:S(2)}) copy-start(bf16[640,512]{1,0:T(8,128)(2,1)S(1)} %collective-permute-done.4.refs_2_) | copy-start | bytes 1966084
  70.5 3.9 %copy-start.6 = (bf16[640,512]{1,0:T(8,128)(2,1)}, bf16[640,512]{1,0:T(8,128)(2,1)S(1)}, u32[]{:S(2)}) copy-start(bf16[640,512]{1,0:T(8,128)(2,1)S(1)} %collective-permute-done.3.refs_1_) | copy-start | bytes 1966084
  70.5 14.7 %collective-permute-start.17 = (bf16[640,512]{1,0:T(8,128)(2,1)S(1)}, bf16[640,512]{1,0:T(8,128)(2,1)S(1)}, u32[]{:S(2)}, u32[]{:S(2)}) collective-permute-start(bf16[640,512]{1,0:T(8,128)(2,1)S(1)} %collective-permute-done.3.refs_1_), channel_id=1, source_target_pairs={{0,32},{32,64},{64,96},{96,128},{128,160},{160,192},{192,224},{224... | collective-permute-start | bytes 1966088 | tf_op jit(solution)/shard_map/ppermute | solution.py:28
  70.5 14.7 %collective-permute-start.18 = (bf16[640,512]{1,0:T(8,128)(2,1)S(1)}, bf16[640,512]{1,0:T(8,128)(2,1)S(1)}, u32[]{:S(2)}, u32[]{:S(2)}) collective-permute-start(bf16[640,512]{1,0:T(8,128)(2,1)S(1)} %collective-permute-done.4.refs_2_), channel_id=1, source_target_pairs={{0,224},{32,0},{64,32},{96,64},{128,96},{160,128},{192,160},{224,1... | collective-permute-start | bytes 1966088 | tf_op jit(solution)/shard_map/ppermute | solution.py:28
  80.5 13.9 %copy-start.11 = (bf16[3,256,128]{2,1,0:T(8,128)(2,1)S(1)}, bf16[3,256,128]{2,1,0:T(8,128)(2,1)}, u32[]{:S(2)}) copy-start(bf16[3,256,128]{2,1,0:T(8,128)(2,1)} %param.12) | copy-start | bytes 589828
  85.2 5.6 %copy-start.3 = (bf16[640,512]{1,0:T(8,128)(2,1)}, bf16[640,512]{1,0:T(8,128)(2,1)S(1)}, u32[]{:S(2)}) copy-start(bf16[640,512]{1,0:T(8,128)(2,1)S(1)} %collective-permute-done.17.refs_0_) | copy-start | bytes 1966084
  85.2 5.6 %copy-start.4 = (bf16[640,512]{1,0:T(8,128)(2,1)}, bf16[640,512]{1,0:T(8,128)(2,1)S(1)}, u32[]{:S(2)}) copy-start(bf16[640,512]{1,0:T(8,128)(2,1)S(1)} %collective-permute-done.18.refs_1_) | copy-start | bytes 1966084
  85.2 14.8 %collective-permute-start.19 = (bf16[640,512]{1,0:T(8,128)(2,1)S(1)}, bf16[640,512]{1,0:T(8,128)(2,1)S(1)}, u32[]{:S(2)}, u32[]{:S(2)}) collective-permute-start(bf16[640,512]{1,0:T(8,128)(2,1)S(1)} %collective-permute-done.17.refs_0_), channel_id=1, source_target_pairs={{0,32},{32,64},{64,96},{96,128},{128,160},{160,192},{192,224},{224... | collective-permute-start | bytes 1966088 | tf_op jit(solution)/shard_map/ppermute | solution.py:28
  85.3 14.8 %collective-permute-start.20 = (bf16[640,512]{1,0:T(8,128)(2,1)S(1)}, bf16[640,512]{1,0:T(8,128)(2,1)S(1)}, u32[]{:S(2)}, u32[]{:S(2)}) collective-permute-start(bf16[640,512]{1,0:T(8,128)(2,1)S(1)} %collective-permute-done.18.refs_1_), channel_id=1, source_target_pairs={{0,224},{32,0},{64,32},{96,64},{128,96},{160,128},{192,160},{224,1... | collective-permute-start | bytes 1966088 | tf_op jit(solution)/shard_map/ppermute | solution.py:28
  90.8 12.6 %collective-permute-start.25 = (bf16[640,512]{1,0:T(8,128)(2,1)S(1)}, bf16[640,512]{1,0:T(8,128)(2,1)S(1)}, u32[]{:S(2)}, u32[]{:S(2)}) collective-permute-start(bf16[640,512]{1,0:T(8,128)(2,1)S(1)} %slice.53), channel_id=1, source_target_pairs={{0,8},{8,16},{16,24},{24,0},{1,9},{9,17},{17,25},{25,1},{2,10},{10... | collective-permute-start | bytes 1966088 | tf_op jit(solution)/shard_map/ppermute | solution.py:28
  93.7 10.7 %collective-permute-start.26 = (bf16[640,512]{1,0:T(8,128)(2,1)S(1)}, bf16[640,512]{1,0:T(8,128)(2,1)}, u32[]{:S(2)}, u32[]{:S(2)}) collective-permute-start(bf16[640,512]{1,0:T(8,128)(2,1)S(1)} %slice.54), channel_id=1, source_target_pairs={{0,24},{8,0},{16,8},{24,16},{1,25},{9,1},{17,9},{25,17},{2,26},{10... | collective-permute-start | bytes 1966088 | tf_op jit(solution)/shard_map/ppermute | solution.py:28
  100.0 13.7 %copy-start.1 = (bf16[640,512]{1,0:T(8,128)(2,1)}, bf16[640,512]{1,0:T(8,128)(2,1)S(1)}, u32[]{:S(2)}) copy-start(bf16[640,512]{1,0:T(8,128)(2,1)S(1)} %collective-permute-done.19.refs_2_) | copy-start | bytes 1966084
  100.0 13.7 %copy-start.2 = (bf16[640,512]{1,0:T(8,128)(2,1)}, bf16[640,512]{1,0:T(8,128)(2,1)S(1)}, u32[]{:S(2)}) copy-start(bf16[640,512]{1,0:T(8,128)(2,1)S(1)} %collective-permute-done.20.refs_3_) | copy-start | bytes 1966084
  100.1 13.7 %collective-permute-start.21 = (bf16[320,512]{1,0:T(8,128)(2,1)S(1)}, bf16[320,512]{1,0:T(8,128)(2,1)S(1)}, u32[]{:S(2)}, u32[]{:S(2)}) collective-permute-start(bf16[320,512]{1,0:T(8,128)(2,1)S(1)} %slice.51), channel_id=1, source_target_pairs={{0,32},{32,64},{64,96},{96,128},{128,160},{160,192},{192,224},{224... | collective-permute-start | bytes 983048 | tf_op jit(solution)/shard_map/ppermute | solution.py:28
  100.2 13.6 %collective-permute-start.22 = (bf16[320,512]{1,0:T(8,128)(2,1)S(1)}, bf16[320,512]{1,0:T(8,128)(2,1)S(1)}, u32[]{:S(2)}, u32[]{:S(2)}) collective-permute-start(bf16[320,512]{1,0:T(8,128)(2,1)S(1)} %slice.52), channel_id=1, source_target_pairs={{0,224},{32,0},{64,32},{96,64},{128,96},{160,128},{192,160},{224,1... | collective-permute-start | bytes 983048 | tf_op jit(solution)/shard_map/ppermute | solution.py:28
  103.4 1.0 copy-start.15
  113.7 0.7 copy-start.8
  114.5 0.7 copy-start.9
  135.2 7.7 %collective-permute-start.27 = (bf16[2,256,128]{2,1,0:T(8,128)(2,1)}, bf16[2,256,128]{2,1,0:T(8,128)(2,1)S(1)}, u32[]{:S(2)}, u32[]{:S(2)}) collective-permute-start(bf16[2,256,128]{2,1,0:T(8,128)(2,1)} %get-tuple-element.53), channel_id=1, source_target_pairs={{0,240},{8,248},{16,0},{24,8},{32,16},{40,24},{48,32},{56,40},{64,... | collective-permute-start | bytes 393224 | tf_op jit(solution)/shard_map/ppermute | solution.py:28
  139.9 5.5 %collective-permute-start.28 = (bf16[2,256,128]{2,1,0:T(8,128)(2,1)}, bf16[2,256,128]{2,1,0:T(8,128)(2,1)S(1)}, u32[]{:S(2)}, u32[]{:S(2)}) collective-permute-start(bf16[2,256,128]{2,1,0:T(8,128)(2,1)} %get-tuple-element.54), channel_id=1, source_target_pairs={{0,248},{8,0},{16,8},{24,16},{32,24},{40,32},{48,40},{56,48},{64,5... | collective-permute-start | bytes 393224 | tf_op jit(solution)/shard_map/ppermute | solution.py:28
  142.6 9.6 %collective-permute-start.29 = (bf16[2,256,128]{2,1,0:T(8,128)(2,1)}, bf16[2,256,128]{2,1,0:T(8,128)(2,1)S(1)}, u32[]{:S(2)}, u32[]{:S(2)}) collective-permute-start(bf16[2,256,128]{2,1,0:T(8,128)(2,1)} %get-tuple-element.55), channel_id=1, source_target_pairs={{0,8},{8,16},{16,24},{24,32},{32,40},{40,48},{48,56},{56,64},{64,7... | collective-permute-start | bytes 393224 | tf_op jit(solution)/shard_map/ppermute | solution.py:28
  142.6 9.9 %collective-permute-start.30 = (bf16[2,256,128]{2,1,0:T(8,128)(2,1)}, bf16[2,256,128]{2,1,0:T(8,128)(2,1)S(1)}, u32[]{:S(2)}, u32[]{:S(2)}) collective-permute-start(bf16[2,256,128]{2,1,0:T(8,128)(2,1)} %get-tuple-element.56), channel_id=1, source_target_pairs={{0,16},{8,24},{16,32},{24,40},{32,48},{40,56},{48,64},{56,72},{64,... | collective-permute-start | bytes 393224 | tf_op jit(solution)/shard_map/ppermute | solution.py:28
Sparse Core Ops, SparseCore 0:
  11.3 52.1 all-gather.1
